TPU v7x, 32 devices: a whole 2x2x4 slice. The times are simulated.
32 devices in a mesh: node: 8 (over y, x, core), edge: 4 (over z).
Axes of the slice: x: 2, y: 2, z: 4, core: 2. Of those that a mesh axis runs over, the one named last changes fastest.
Arguments:
- embed: bfloat16 [8192, 256], P('node'), may hold values from -6 to 6
- cotangent: bfloat16 [8192, 256], P('node'), may hold values from -6 to 6
- values: bfloat16 [8, 4, 128, 128, 128], P('node', 'edge'), may hold values from 0.0023345947 to 0.0390625
- block_slot: int32 [8, 4, 128], P('node', 'edge'), may hold values from 0 to 7
- block_col: int32 [8, 4, 128], P('node', 'edge'), may hold values from 0 to 7
- block_count: int32 [8, 4], P('node', 'edge'), may hold values from 16 to 128, as said below
- slot_rows: int32 [8, 8], P('node'), may hold values from 0 to 7
Outputs:
- final: bfloat16 [8192, 256], P(('node', 'edge'))
- grad: bfloat16 [8192, 256], P(('node', 'edge'))
Inputs may be any that keep to these rules, and one draw needn't show every extreme that they name: `block_count`: slots at and past a device's count are padding. Some device uses all 128 slots in every draw.
All inputs are finite; a program needn't handle non-finite values.
Results may differ from a plain program's by a relative error of at most 0.0026.
Values may be sent and summed in bfloat16 or wider, within the bound.
A program may use at most 128 MiB of HBM per device.

v0:
```python
import jax
import jax.numpy as jnp
from jax import lax
from jax.sharding import PartitionSpec as P

D = 256
BS = 128
LAYERS = 2


turn_blocks = 16


def edge_total(terms):
    return lax.psum_scatter(terms, "edge", scatter_dimension=1, tiled=True)


def share(shard):
    return lax.all_gather(shard, "edge", axis=0, tiled=True)


def prepare(values, block_slot, block_col, block_count):
    vals = values[0, 0]
    slots = block_slot[0, 0]
    cols = block_col[0, 0]
    count = block_count[0, 0]
    total = vals.shape[0]
    turns = total // turn_blocks
    return (vals, slots, cols, count, turns)


def run_blocks(carry, blocks, kernel):
    vals, slots, cols, active, turns = blocks

    def step(turn, acc):
        begin = turn * turn_blocks
        vals_part = lax.dynamic_slice_in_dim(vals, begin, turn_blocks, 0)
        slot_part = lax.dynamic_slice_in_dim(slots, begin, turn_blocks, 0)
        col_part = lax.dynamic_slice_in_dim(cols, begin, turn_blocks, 0)
        live = begin + jnp.arange(turn_blocks, dtype=jnp.int32) < active
        return kernel(acc, vals_part, slot_part, col_part, live)

    return lax.fori_loop(0, turns, step, carry)


def forward_kernel(source):

    def kernel(acc, vals_part, slot_part, col_part, live):
        picked = source[col_part]
        prods = jnp.einsum("bij,bjd->bid", vals_part, picked, preferred_element_type=jnp.float32)
        prods = jnp.where(live[:, None, None], prods, 0.0)
        return acc.at[slot_part].add(prods)

    return kernel


def backward_kernel(wanted):

    def kernel(acc, vals_part, slot_part, col_part, live):
        picked = wanted[slot_part]
        prods = jnp.einsum("bij,bid->bjd", vals_part, picked, preferred_element_type=jnp.float32)
        prods = jnp.where(live[:, None, None], prods, 0.0)
        return acc.at[col_part].add(prods)

    return kernel


def forward_layer(group_rows, blocks, slot_index):
    groups = group_rows.shape[0] // BS
    source = group_rows.reshape(BS, groups, D).transpose(1, 0, 2)
    empty = jnp.zeros((slot_index.shape[0], BS, D), jnp.float32)
    parts = run_blocks(empty, blocks, forward_kernel(source))
    arrived = lax.all_to_all(parts, "node", split_axis=0, concat_axis=0, tiled=True)
    placed = jnp.zeros((groups,) + arrived.shape[1:], jnp.float32).at[slot_index].add(arrived)
    placed = edge_total(placed)
    return placed.transpose(1, 0, 2).reshape(-1, D)


def backward_layer(group_rows, blocks, slot_index):
    groups = group_rows.shape[0] // BS
    grad_blocks = group_rows.reshape(BS, groups, D).transpose(1, 0, 2)
    outgoing = grad_blocks[slot_index]
    wanted = lax.all_to_all(outgoing, "node", split_axis=0, concat_axis=0, tiled=True)
    empty = jnp.zeros((groups, BS, D), jnp.float32)
    summed = run_blocks(empty, blocks, backward_kernel(wanted))
    reduced = edge_total(summed)
    return reduced.transpose(1, 0, 2).reshape(-1, D)


def propagate(start_rows, layer_fn, blocks, slot_index):
    width = lax.axis_size("edge")
    place = lax.axis_index("edge")
    share_len = start_rows.shape[0] // width
    current = start_rows
    total = lax.dynamic_slice_in_dim(start_rows, place * share_len, share_len, 0).astype(
        jnp.float32
    )
    for layer in range(LAYERS):
        shard = layer_fn(current, blocks, slot_index)
        if layer + 1 < LAYERS:
            rounded = lax.optimization_barrier(shard.astype(jnp.bfloat16))
            total = total + rounded.astype(jnp.float32)
            current = share(rounded)
        else:
            total = total + shard
    return (total / float(LAYERS + 1)).astype(jnp.bfloat16)


def shards(embed, cotangent, values, block_slot, block_col, block_count, slot_rows):
    blocks = prepare(values, block_slot, block_col, block_count)
    slot_index = slot_rows[0]
    final = propagate(embed, forward_layer, blocks, slot_index)
    grad = propagate(cotangent, backward_layer, blocks, slot_index)
    return (final, grad)


def solution(mesh):
    placed = (
        P("node", None),
        P("node", None),
        P("node", "edge", None, None, None),
        P("node", "edge", None),
        P("node", "edge", None),
        P("node", "edge"),
        P("node", None),
    )
    return jax.shard_map(
        shards,
        mesh=mesh,
        in_specs=placed,
        out_specs=(P(("node", "edge"), None), P(("node", "edge"), None)),
        check_vma=False,
    )
```

profile of v0, /device:TPU:8, one launch (start us, length us, event | category | flops | bytes accessed | tf_op | source)
XLA Modules:
  0.0 385.1 jit_solution(8088732756860100239)
XLA Ops:
  10.4 4.1 %all-to-all-start.2 = ((bf16[8,128,256]{2,1,0:T(8,128)(2,1)}), bf16[8,128,256]{2,1,0:T(8,128)(2,1)}, u32[]{:S(2)}, u32[]{:S(2)}) async-start(bf16[8,128,256]{2,1,0:T(8,128)(2,1)} %gather_fusion.4), calls=%async_computation.4 | async-start | bytes 1048576 | tf_op jit(solution)/shard_map/all_to_all | solution.py:83
  14.6 6.4 %copy.26 = bf16[1,1,128,128,128]{3,4,2,1,0:T(8,128)(2,1)} copy(bf16[1,1,128,128,128]{4,3,2,1,0:T(8,128)(2,1)} %param.17) | data formatting | bytes 8388608 | tf_op args[2]
  24.4 59.5 %while.54 = (s32[]{:T(128)}, f32[8,128,256]{2,1,0:T(8,128)S(1)}, s32[128]{0:T(128)S(1)}, s32[]{:T(128)}, bf16[128,128,128]{1,2,0:T(8,128)(2,1)}, /*index=5*/s32[...) while((s32[]{:T(128)}, f32[8,128,256]{2,1,0:T(8,128)S(1)}, ...), condition=%wide.region_12.13_spmd, body=%wide.region_10.12_spmd.sunk | while | flops 135267456 | bytes 12063371 | solution.py:43
  24.5 2.7 gather_fusion.2
  31.9 2.7 gather_fusion.2
  39.4 2.7 gather_fusion.2
  46.8 2.7 gather_fusion.2
  54.3 2.7 gather_fusion.2
  61.7 2.7 gather_fusion.2
  69.1 2.7 gather_fusion.2
  76.6 2.7 gather_fusion.2
  86.0 66.0 %while.52 = (s32[]{:T(128)}, f32[8,128,256]{2,1,0:T(8,128)}, s32[128]{0:T(128)S(1)}, s32[]{:T(128)}, bf16[128,128,128]{2,1,0:T(8,128)(2,1)}, /*index=5*/s32[128]...) while((s32[]{:T(128)}, f32[8,128,256]{2,1,0:T(8,128)}, ...), condition=%wide.region_2.3_spmd, body=%wide.region_0.2_spmd.sunk | while | flops 135267456 | bytes 12063371 | solution.py:43
  89.9 4.3 %scatter_fusion = f32[8,128,256]{2,1,0:T(8,128)} fusion(f32[8,128,256]{2,1,0:T(8,128)} %get-tuple-element.808, s32[16]{0:T(128)S(1)} %get-tuple-element.767, f32[16,128,256]{2,1,0:T(8,128)S(1)} %convolution_select_fusion.8), kind=kCustom, calls=%fused_computation.6.clone.1 | custom fusion | flops 524288 | bytes 6291520 | tf_op jit(solution)/shard_map/while/body/eval_jaxpr/scatter-add | solution.py:52
  98.1 4.3 %scatter_fusion = f32[8,128,256]{2,1,0:T(8,128)} fusion(f32[8,128,256]{2,1,0:T(8,128)} %get-tuple-element.808, s32[16]{0:T(128)S(1)} %get-tuple-element.767, f32[16,128,256]{2,1,0:T(8,128)S(1)} %convolution_select_fusion.8), kind=kCustom, calls=%fused_computation.6.clone.1 | custom fusion | flops 524288 | bytes 6291520 | tf_op jit(solution)/shard_map/while/body/eval_jaxpr/scatter-add | solution.py:52
  106.3 4.4 %scatter_fusion = f32[8,128,256]{2,1,0:T(8,128)} fusion(f32[8,128,256]{2,1,0:T(8,128)} %get-tuple-element.808, s32[16]{0:T(128)S(1)} %get-tuple-element.767, f32[16,128,256]{2,1,0:T(8,128)S(1)} %convolution_select_fusion.8), kind=kCustom, calls=%fused_computation.6.clone.1 | custom fusion | flops 524288 | bytes 6291520 | tf_op jit(solution)/shard_map/while/body/eval_jaxpr/scatter-add | solution.py:52
  114.5 4.4 %scatter_fusion = f32[8,128,256]{2,1,0:T(8,128)} fusion(f32[8,128,256]{2,1,0:T(8,128)} %get-tuple-element.808, s32[16]{0:T(128)S(1)} %get-tuple-element.767, f32[16,128,256]{2,1,0:T(8,128)S(1)} %convolution_select_fusion.8), kind=kCustom, calls=%fused_computation.6.clone.1 | custom fusion | flops 524288 | bytes 6291520 | tf_op jit(solution)/shard_map/while/body/eval_jaxpr/scatter-add | solution.py:52
  122.8 4.4 %scatter_fusion = f32[8,128,256]{2,1,0:T(8,128)} fusion(f32[8,128,256]{2,1,0:T(8,128)} %get-tuple-element.808, s32[16]{0:T(128)S(1)} %get-tuple-element.767, f32[16,128,256]{2,1,0:T(8,128)S(1)} %convolution_select_fusion.8), kind=kCustom, calls=%fused_computation.6.clone.1 | custom fusion | flops 524288 | bytes 6291520 | tf_op jit(solution)/shard_map/while/body/eval_jaxpr/scatter-add | solution.py:52
  131.0 4.3 %scatter_fusion = f32[8,128,256]{2,1,0:T(8,128)} fusion(f32[8,128,256]{2,1,0:T(8,128)} %get-tuple-element.808, s32[16]{0:T(128)S(1)} %get-tuple-element.767, f32[16,128,256]{2,1,0:T(8,128)S(1)} %convolution_select_fusion.8), kind=kCustom, calls=%fused_computation.6.clone.1 | custom fusion | flops 524288 | bytes 6291520 | tf_op jit(solution)/shard_map/while/body/eval_jaxpr/scatter-add | solution.py:52
  139.2 4.6 %scatter_fusion = f32[8,128,256]{2,1,0:T(8,128)} fusion(f32[8,128,256]{2,1,0:T(8,128)} %get-tuple-element.808, s32[16]{0:T(128)S(1)} %get-tuple-element.767, f32[16,128,256]{2,1,0:T(8,128)S(1)} %convolution_select_fusion.8), kind=kCustom, calls=%fused_computation.6.clone.1 | custom fusion | flops 524288 | bytes 6291520 | tf_op jit(solution)/shard_map/while/body/eval_jaxpr/scatter-add | solution.py:52
  147.6 4.3 %scatter_fusion = f32[8,128,256]{2,1,0:T(8,128)} fusion(f32[8,128,256]{2,1,0:T(8,128)} %get-tuple-element.808, s32[16]{0:T(128)S(1)} %get-tuple-element.767, f32[16,128,256]{2,1,0:T(8,128)S(1)} %convolution_select_fusion.8), kind=kCustom, calls=%fused_computation.6.clone.1 | custom fusion | flops 524288 | bytes 6291520 | tf_op jit(solution)/shard_map/while/body/eval_jaxpr/scatter-add | solution.py:52
  152.0 3.6 all-to-all-start
  156.6 16.5 %all_gather.7 = bf16[1024,256]{1,0:T(8,128)(2,1)S(1)} all-gather(bf16[256,256]{1,0:T(8,128)(2,1)S(1)} %bitcast.67), channel_id=1, replica_groups=mesh['node'=8,'edge'=4] {'edge'}, dimensions={0}, use_global_device_ids=true | all-gather | bytes 655360 | tf_op jit(solution)/shard_map/all_gather | solution.py:19
  174.7 4.2 %all-to-all-start.3 = ((bf16[8,128,256]{2,1,0:T(8,128)(2,1)}), bf16[8,128,256]{2,1,0:T(8,128)(2,1)}, u32[]{:S(2)}, u32[]{:S(2)}) async-start(bf16[8,128,256]{2,1,0:T(8,128)(2,1)} %gather_fusion.5), calls=%async_computation.6 | async-start | bytes 1048576 | tf_op jit(solution)/shard_map/all_to_all | solution.py:83
  181.3 7.3 %all-to-all-done.3 = bf16[8,128,256]{2,1,0:T(8,128)(2,1)} async-done(((bf16[8,128,256]{2,1,0:T(8,128)(2,1)}), bf16[8,128,256]{2,1,0:T(8,128)(2,1)}, u32[]{:S(2)}, u32[]{:S(2)}) %all-to-all-start.3) | async-done | bytes 524320 | tf_op jit(solution)/shard_map/all_to_all | solution.py:83
  188.8 59.5 %while.55 = (s32[]{:T(128)}, f32[8,128,256]{2,1,0:T(8,128)S(1)}, s32[128]{0:T(128)S(1)}, s32[]{:T(128)}, bf16[128,128,128]{1,2,0:T(8,128)(2,1)}, /*index=5*/s32[...) while((s32[]{:T(128)}, f32[8,128,256]{2,1,0:T(8,128)S(1)}, ...), condition=%wide.region_16.17_spmd, body=%wide.region_14.16_spmd.sunk | while | flops 135267456 | bytes 12063371 | solution.py:43
  188.9 2.7 gather_fusion.3
  196.3 2.6 gather_fusion.3
  250.4 19.5 %all_gather.6 = bf16[1024,256]{1,0:T(8,128)(2,1)S(1)} all-gather(bf16[256,256]{1,0:T(8,128)(2,1)S(1)} %bitcast.69), channel_id=1, replica_groups=mesh['node'=8,'edge'=4] {'edge'}, dimensions={0}, use_global_device_ids=true | all-gather | bytes 655360 | tf_op jit(solution)/shard_map/all_gather | solution.py:19
  270.9 59.5 %while.53 = (s32[]{:T(128)}, f32[8,128,256]{2,1,0:T(8,128)S(1)}, s32[128]{0:T(128)S(1)}, s32[]{:T(128)}, bf16[128,128,128]{2,1,0:T(8,128)(2,1)}, /*index=5*/s32[...) while((s32[]{:T(128)}, f32[8,128,256]{2,1,0:T(8,128)S(1)}, ...), condition=%wide.region_7.8_spmd, body=%wide.region_5.7_spmd.sunk | while | flops 135267456 | bytes 12063371 | solution.py:43
  271.0 2.6 gather_fusion.1
  330.4 19.0 %all_to_all.20 = f32[8,128,256]{2,1,0:T(8,128)S(1)} all-to-all(f32[8,128,256]{2,1,0:T(8,128)S(1)} %get-tuple-element.499), channel_id=1, replica_groups=mesh['node'=8,'edge'=4] {'node'}, dimensions={0} | all-to-all | bytes 2097152 | tf_op jit(solution)/shard_map/all_to_all | solution.py:73
  353.7 23.0 %reduce-scatter.7.cloned.1.call-done = f32[8,32,256]{2,1,0:T(8,128)} async-done(((f32[8,128,256]{2,1,0:T(8,128)}), f32[8,32,256]{2,1,0:T(8,128)}) %reduce-scatter.7.cloned.1.call-update) | async-done | bytes 262160 | tf_op jit(solution)/shard_map/reduce_scatter | solution.py:15
  (222 shorter events, 202.2 us)
Async XLA Ops:
  10.4 13.9 %all-to-all-start.2 = ((bf16[8,128,256]{2,1,0:T(8,128)(2,1)}), bf16[8,128,256]{2,1,0:T(8,128)(2,1)}, u32[]{:S(2)}, u32[]{:S(2)}) async-start(bf16[8,128,256]{2,1,0:T(8,128)(2,1)} %gather_fusion.4), calls=%async_computation.4 | async-start | bytes 1048576 | tf_op jit(solution)/shard_map/all_to_all | solution.py:83
  14.5 141.1 %reduce-scatter.9.cloned.1.call-start = ((), (), s32[]{:S(2)}) async-start(), calls=%async_computation.10 | async-start | bytes 1310720 | tf_op jit(solution)/shard_map/reduce_scatter | solution.py:15
  14.6 6.5 %copy-start.4 = (bf16[1024,256]{1,0:T(8,128)(2,1)S(1)}, bf16[1024,256]{1,0:T(8,128)(2,1)}, u32[]{:S(2)}) copy-start(bf16[1024,256]{1,0:T(8,128)(2,1)} %param.15) | copy-start | bytes 1572868
  21.0 3.3 copy-start.5
  21.0 3.4 copy-start.6
  83.9 1.0 copy-start
  152.0 22.7 %all-to-all-start = ((f32[8,128,256]{2,1,0:T(8,128)}), f32[8,128,256]{2,1,0:T(8,128)S(1)}, u32[]{:S(2)}, u32[]{:S(2)}) async-start(f32[8,128,256]{2,1,0:T(8,128)} %get-tuple-element.498), calls=%async_computation | async-start | bytes 2097152 | tf_op jit(solution)/shard_map/all_to_all | solution.py:73
  174.7 14.0 %all-to-all-start.3 = ((bf16[8,128,256]{2,1,0:T(8,128)(2,1)}), bf16[8,128,256]{2,1,0:T(8,128)(2,1)}, u32[]{:S(2)}, u32[]{:S(2)}) async-start(bf16[8,128,256]{2,1,0:T(8,128)(2,1)} %gather_fusion.5), calls=%async_computation.6 | async-start | bytes 1048576 | tf_op jit(solution)/shard_map/all_to_all | solution.py:83
  178.8 70.5 %reduce-scatter.5.cloned.1.call-start = ((), (), s32[]{:S(2)}) async-start(), calls=%async_computation.8 | async-start | bytes 1310720 | tf_op jit(solution)/shard_map/reduce_scatter | solution.py:15
  180.3 1.0 copy-start.3
  181.3 170.6 %reduce-scatter.11.cloned.1.call-start = ((), (), s32[]{:S(2)}) async-start(), calls=%async_computation.11 | async-start | bytes 1310720 | tf_op jit(solution)/shard_map/reduce_scatter | solution.py:15
  248.2 1.0 copy-start.1
  249.2 127.5 %reduce-scatter.7.cloned.1.call-start = ((), (), s32[]{:S(2)}) async-start(), calls=%async_computation.9 | async-start | bytes 1310720 | tf_op jit(solution)/shard_map/reduce_scatter | solution.py:15
  350.9 1.0 copy-start.2
Sparse Core Ops, SparseCore 0:
  85.0 24.3 reduce-scatter.8
  182.1 26.6 reduce-scatter.4
  249.4 30.2 reduce-scatter.10
  352.0 24.6 reduce-scatter.6
where the time goes:
time: 393 us; the launch traced here: 385 us
  other arithmetic  120 us (31%)
  local copies, waits for them, and re-layouts  94.6 us (24%)
  matrix products  55.3 us (14%)
  blocking collectives  55.1 us (14%)
  waiting for transfers between devices  32.8 us (8%)
  between operations  14 us (4%)
  starting transfers between devices  12 us (3%)
    scatter-add x16, other arithmetic, kernel(): return acc.at[slot_part].add(prods)  52.5 us
    gather x16, local copies, waits for them, and re-layouts, kernel(): picked = wanted[slot_part]  42.4 us
    all_gather x2, blocking collectives, share(): return lax.all_gather(shard, 'edge', axis=0, tiled=True)  36.1 us
    scatter-add x16, other arithmetic, kernel(): return acc.at[col_part].add(prods)  35.2 us
    gather x16, local copies, waits for them, and re-layouts, kernel(): picked = source[col_part]  34.4 us
    dot_general x16, matrix products, kernel(): jnp.einsum('bij,bid->bjd', vals_part, picked, preferred_element_type=jnp....  29 us
    dot_general x16, matrix products, kernel(): jnp.einsum('bij,bjd->bid', vals_part, picked, preferred_element_type=jnp....  26.3 us
    reduce_scatter x4, waiting for transfers between devices, edge_total(): return lax.psum_scatter(terms, 'edge', scatter_dimension=1, tiled=True)  23.1 us
  transfers between devices with their start and end apart: 7, of which 3 were waited for; matrix products, arithmetic and copies ran while one was open for 52% of the time, Pallas kernels for 0%

commit v1 on v0

v1 whole, which is shorter than its diff:
```python
import jax
import jax.numpy as jnp
from jax import lax
from jax.experimental import pallas as pl
from jax.experimental.pallas import tpu as pltpu
from jax.sharding import PartitionSpec as P

LAYERS = 2
CHUNK = 16


def dense_kernel(slots_ref, cols_ref, count_ref, vals_ref, out_ref, acc):
    turn = pl.program_id(0)
    groups, sources, size, _ = acc.shape
    width, _, part, _ = out_ref.shape

    @pl.when(turn == 0)
    def _():
        acc[...] = jnp.zeros_like(acc)

    begin = turn * CHUNK
    live = jnp.clip(count_ref[0] - begin, 0, CHUNK)

    def add(b, carry):
        s, c = slots_ref[begin + b], cols_ref[begin + b]
        acc[s, c] += vals_ref[b].astype(jnp.float32)
        return carry

    lax.fori_loop(0, live, add, 0)

    @pl.when(turn == pl.num_programs(0) - 1)
    def _():
        def put(s, carry):
            for c in range(sources):
                for e in range(width):
                    out_ref[e, s, :, c * size:(c + 1) * size] = acc[
                        s, c, e * part:(e + 1) * part, :
                    ].astype(out_ref.dtype)
            return carry

        lax.fori_loop(0, groups, put, 0)


def dense_adjacency(vals, slots, cols, count, groups, sources, width):
    total, size, _ = vals.shape
    part = size // width
    return pl.pallas_call(
        dense_kernel,
        out_shape=jax.ShapeDtypeStruct((width, groups, part, sources * size), jnp.bfloat16),
        grid_spec=pltpu.PrefetchScalarGridSpec(
            num_scalar_prefetch=3,
            grid=(total // CHUNK,),
            in_specs=[pl.BlockSpec((CHUNK, size, size), lambda t, *_: (t, 0, 0))],
            out_specs=pl.BlockSpec(
                (width, groups, part, sources * size), lambda t, *_: (0, 0, 0, 0)
            ),
            scratch_shapes=[pltpu.VMEM((groups, sources, size, size), jnp.float32)],
        ),
        compiler_params=pltpu.CompilerParams(
            dimension_semantics=("arbitrary",), vmem_limit_bytes=56 * 1024 * 1024
        ),
    )(slots, cols, count, vals)


def shards(embed, cotangent, values, block_slot, block_col, block_count, slot_rows):
    width = lax.axis_size("edge")
    place = lax.axis_index("edge")
    groups = slot_rows.shape[1]
    vals = values[0, 0]
    size = vals.shape[1]
    part = size // width
    sources = embed.shape[0] // size
    depth = embed.shape[1]
    slot_index = slot_rows[0]

    dense = dense_adjacency(
        vals, block_slot[0, 0], block_col[0, 0], block_count[0], groups, sources, width
    )
    dense = dense.reshape(width * groups * part, sources * size)

    def share_of(rows):
        rows = lax.dynamic_slice_in_dim(rows, place * (sources * part), sources * part, 0)
        return rows.reshape(part, sources, depth).transpose(1, 0, 2)

    def forward(source):
        return jnp.dot(
            dense, source.reshape(sources * size, depth), preferred_element_type=jnp.float32
        ).reshape(width, groups * part, depth)

    def backward(wanted):
        out = lax.dot_general(
            dense,
            wanted.reshape(width * groups * part, depth),
            (((0,), (0,)), ((), ())),
            preferred_element_type=jnp.float32,
        )
        out = out.reshape(sources, width, part, depth).transpose(1, 0, 2, 3)
        return out.reshape(width, sources * part, depth)

    def place_rows(arrived):
        hit = slot_index[None, :] == jnp.arange(sources, dtype=jnp.int32)[:, None]
        terms = jnp.where(hit[:, :, None, None], arrived.astype(jnp.float32)[None], 0.0)
        return terms.sum(1)

    def exchange(x):
        return lax.all_to_all(x, "node", split_axis=0, concat_axis=0, tiled=True)

    embed_share, cot_share = share_of(embed), share_of(cotangent)

    wanted = lax.all_gather(exchange(cot_share[slot_index]), "edge", axis=0)
    source = embed.reshape(size, sources, depth).transpose(1, 0, 2)

    sums = jnp.concatenate([forward(source), backward(wanted)], axis=1).astype(jnp.bfloat16)
    sums = lax.psum_scatter(sums, "edge", scatter_dimension=0, tiled=False)
    parts = sums[: groups * part].reshape(groups, part, depth)
    back = sums[groups * part:].reshape(sources, part, depth)
    arrived = exchange(jnp.stack([parts, back[slot_index]], axis=1))
    layer = place_rows(arrived[:, 0]).astype(jnp.bfloat16)
    gathered = lax.all_gather(
        jnp.concatenate([layer, arrived[:, 1]], axis=0), "edge", axis=0
    )
    source = gathered[:, :sources].transpose(1, 0, 2, 3)
    wanted = gathered[:, sources:]

    sums = jnp.concatenate([forward(source), backward(wanted)], axis=1)
    sums = lax.psum_scatter(sums, "edge", scatter_dimension=0, tiled=False)
    top = place_rows(exchange(sums[: groups * part].reshape(groups, part, depth)))
    top_back = sums[groups * part:].reshape(sources, part, depth)

    def mean(first, second, third):
        total = first.astype(jnp.float32) + second.astype(jnp.float32) + third
        total = (total / float(LAYERS + 1)).astype(jnp.bfloat16)
        return total.transpose(1, 0, 2).reshape(part * sources, depth)

    return mean(embed_share, layer, top), mean(cot_share, back, top_back)


def solution(mesh):
    placed = (
        P("node", None),
        P("node", None),
        P("node", "edge", None, None, None),
        P("node", "edge", None),
        P("node", "edge", None),
        P("node", "edge"),
        P("node", None),
    )
    return jax.shard_map(
        shards,
        mesh=mesh,
        in_specs=placed,
        out_specs=(P(("node", "edge"), None), P(("node", "edge"), None)),
        check_vma=False,
    )
```

time: 393 us -> 187 us (0.48)
  the two profiles are of different devices: /device:TPU:8 before, /device:TPU:0 now
where the time goes in v1:
time: 187 us; the launch traced here: 186 us
  waiting for transfers between devices  109 us (58%)
  blocking collectives  15.9 us (9%)
  between operations  14.6 us (8%)
  local copies, waits for them, and re-layouts  13.8 us (7%)
  starting transfers between devices  12.6 us (7%)
  Pallas kernels  8 us (4%)
  matrix products  6.17 us (3%)
  other arithmetic  5.62 us (3%)
    reduce_scatter x2, waiting for transfers between devices, shards(): sums = lax.psum_scatter(sums, 'edge', scatter_dimension=0, tiled=False)  71.3 us
    all_gather x1, waiting for transfers between devices, shards(): lax.all_gather(jnp.concatenate([layer, arrived[:, 1]], axis=0), 'edge', a...  24.9 us
    all_gather x1, blocking collectives, shards(): wanted = lax.all_gather(exchange(cot_share[slot_index]), 'edge', axis=0)  15.9 us
    all_to_all x3, waiting for transfers between devices, exchange(): return lax.all_to_all(x, 'node', split_axis=0, concat_axis=0, tiled=True)  13 us
    all_to_all x3, starting transfers between devices, exchange(): return lax.all_to_all(x, 'node', split_axis=0, concat_axis=0, tiled=True)  12.5 us
    pallas_call x1, Pallas kernels, dense_adjacency(): pl.pallas_call(dense_kernel, out_shape=jax.ShapeDtypeStruct((width, group...  8 us
  transfers between devices with their start and end apart: 6, of which 5 were waited for; matrix products, arithmetic and copies ran while one was open for 4% of the time, Pallas kernels for 4%

profile of v1, /device:TPU:0, one launch (start us, length us, event | category | flops | bytes accessed | tf_op | source)
XLA Modules:
  0.0 185.9 jit_solution(15794173428877005087)
XLA Ops:
  7.2 1.0 copy-done
  8.3 0.7 fusion.5
  8.9 1.2 gather_fusion
  10.1 5.2 %all-to-all-start = ((bf16[8,32,256]{2,1,0:T(8,128)(2,1)}), bf16[8,32,256]{2,1,0:T(8,128)(2,1)S(1)}, u32[]{:S(2)}, u32[]{:S(2)}) async-start(bf16[8,32,256]{2,1,0:T(8,128)(2,1)} %gather_fusion), calls=%async_computation | async-start | bytes 262144 | tf_op jit(solution)/shard_map/all_to_all | solution.py:106
  16.0 1.1 copy.52
  17.1 8.0 %shard_map.86 = bf16[4,8,32,1024]{3,2,1,0:T(8,128)(2,1)} custom-call(s32[128]{0:T(128)} %bitcast.115, s32[128]{0:T(128)} %bitcast.116, s32[1]{0:T(128)} %bitcast.92.count_ref, bf16[128,128,128]{2,1,0:T(8,128)(2,1)} %bitcast.96), custom_call_target="tpu_custom_call" | custom-call | tf_op jit(solution)/shard_map/pallas_call | solution.py:47
  25.1 2.4 %convolution_convert_fusion.1 = bf16[4,256,256]{2,1,0:T(8,128)(2,1)S(1)} fusion(bf16[4,256,1024]{2,1,0:T(8,128)(2,1)} %bitcast.93, bf16[1024,256,1]{1,0,2:T(8,128)(2,1)S(1)} %bitcast.108), kind=kOutput, calls=%fused_computation.7 | convolution fusion | flops 537133056 | bytes 3145728 | tf_op jit(solution)/shard_map/dot_general | solution.py:86
  27.6 2.6 %copy.53 = bf16[1024,1024]{1,0:T(8,128)(2,1)} copy(bf16[1024,1024]{0,1:T(8,128)(2,1)S(1)} %bitcast.94) | data formatting | bytes 4194304 | tf_op jit(solution)/shard_map/dot_general | solution.py:91
  30.2 15.9 %all-gather = bf16[32,32,256]{2,1,0:T(8,128)(2,1)S(1)} all-gather(bf16[8,32,256]{2,1,0:T(8,128)(2,1)S(1)} %all-to-all-done), channel_id=2, replica_groups=mesh['node'=8,'edge'=4] {'edge'}, dimensions={0}, use_global_device_ids=true | all-gather | bytes 655360 | tf_op jit(solution)/shard_map/all_gather | solution.py:110
  46.1 2.3 %fusion = bf16[4,8,32,256]{3,2,0,1:T(8,128)(2,1)S(1)} fusion(bf16[8,4,32,1024]{3,2,1,0:T(8,128)(2,1)} %bitcast.99, bf16[1024,256,1,1]{1,0,3,2:T(8,128)(2,1)S(1)} %bitcast.107), kind=kOutput, calls=%fused_computation.8 | convolution fusion | flops 537133056 | bytes 3145728 | tf_op jit(solution)/shard_map/dot_general | solution.py:91
  48.4 1.1 pad_maximum_fusion.1
  49.5 28.7 %reduce-scatter.3.cloned.1.call-done = bf16[1,512,256]{2,1,0:T(8,128)(2,1)} async-done(((bf16[4,512,256]{2,1,0:T(8,128)(2,1)}), bf16[1,512,256]{2,1,0:T(8,128)(2,1)}) %reduce-scatter.3.cloned.1.call-update) | async-done | bytes 262160 | tf_op jit(solution)/shard_map/reduce_scatter | solution.py:114
  78.2 1.0 fusion.8
  79.2 0.6 gather_fusion.1
  79.8 0.7 copy.56
  80.5 3.7 %all-to-all-start.1 = ((bf16[8,2,32,256]{3,2,1,0:T(8,128)(2,1)}), bf16[8,2,32,256]{3,2,1,0:T(8,128)(2,1)S(1)}, u32[]{:S(2)}, u32[]{:S(2)}) async-start(bf16[8,2,32,256]{3,2,1,0:T(8,128)(2,1)} %copy.56), calls=%async_computation.2 | async-start | bytes 524288 | tf_op jit(solution)/shard_map/all_to_all | solution.py:106
  84.3 6.9 %all-to-all-done.1 = bf16[8,2,32,256]{3,2,1,0:T(8,128)(2,1)S(1)} async-done(((bf16[8,2,32,256]{3,2,1,0:T(8,128)(2,1)}), bf16[8,2,32,256]{3,2,1,0:T(8,128)(2,1)S(1)}, u32[]{:S(2)}, u32[]{:S(2)}) %all-to-all-start.1) | async-done | bytes 262176 | tf_op jit(solution)/shard_map/all_to_all | solution.py:106
  91.2 0.2 select_reduce_fusion.1
  91.4 0.7 pad_maximum_fusion.3
  92.2 24.9 %all-gather.4.cloned.1.call-done = bf16[64,32,256]{2,1,0:T(8,128)(2,1)} async-done(((bf16[16,32,256]{2,1,0:T(8,128)(2,1)}), bf16[64,32,256]{2,1,0:T(8,128)(2,1)}) %all-gather.4.cloned.1.call-update) | async-done | bytes 1048592 | tf_op jit(solution)/shard_map/all_gather | solution.py:119
  117.1 1.3 fusion.6
  118.5 0.7 fusion.9
  119.2 0.9 copy-done.2
  120.1 0.7 convolution_bitcast_fusion
  120.9 1.5 pad_maximum_fusion
  122.4 0.9 bitcast_convert_fusion
  123.4 42.6 %reduce-scatter.5.cloned.1.call-done = f32[1,512,256]{2,1,0:T(8,128)} async-done(((f32[4,512,256]{2,1,0:T(8,128)}), f32[1,512,256]{2,1,0:T(8,128)}) %reduce-scatter.5.cloned.1.call-update) | async-done | bytes 524304 | tf_op jit(solution)/shard_map/reduce_scatter | solution.py:126
  166.0 1.8 fusion.7
  167.7 3.6 %all-to-all-start.2 = ((f32[8,32,256]{2,1,0:T(8,128)}), f32[8,32,256]{2,1,0:T(8,128)S(1)}, u32[]{:S(2)}, u32[]{:S(2)}) async-start(f32[8,32,256]{2,1,0:T(8,128)} %bitcast.38), calls=%async_computation.4 | async-start | bytes 524288 | tf_op jit(solution)/shard_map/all_to_all | solution.py:106
  171.4 0.7 copy.73
  172.1 6.1 %all-to-all-done.2 = f32[8,32,256]{2,1,0:T(8,128)S(1)} async-done(((f32[8,32,256]{2,1,0:T(8,128)}), f32[8,32,256]{2,1,0:T(8,128)S(1)}, u32[]{:S(2)}, u32[]{:S(2)}) %all-to-all-start.2) | async-done | bytes 262176 | tf_op jit(solution)/shard_map/all_to_all | solution.py:106
  178.7 0.7 copy.74
  (25 shorter events, 0.9 us)
Async XLA Ops:
  7.2 1.0 copy-start
  10.1 20.1 %all-to-all-start = ((bf16[8,32,256]{2,1,0:T(8,128)(2,1)}), bf16[8,32,256]{2,1,0:T(8,128)(2,1)S(1)}, u32[]{:S(2)}, u32[]{:S(2)}) async-start(bf16[8,32,256]{2,1,0:T(8,128)(2,1)} %gather_fusion), calls=%async_computation | async-start | bytes 262144 | tf_op jit(solution)/shard_map/all_to_all | solution.py:106
  15.3 62.9 %reduce-scatter.3.cloned.1.call-start = ((), (), s32[]{:S(2)}) async-start(), calls=%async_computation.5 | async-start | bytes 1310720 | tf_op jit(solution)/shard_map/reduce_scatter | solution.py:114
  25.1 2.5 %copy-start.1 = (bf16[4,8,32,1024]{3,2,1,0:T(8,128)(2,1)S(1)}, bf16[4,8,32,1024]{3,2,1,0:T(8,128)(2,1)}, u32[]{:S(2)}) copy-start(bf16[4,8,32,1024]{3,2,1,0:T(8,128)(2,1)} %shard_map.86) | copy-start | bytes 6291460
  49.5 34.8 %copy-start.3 = (s32[1,8]{1,0:T(1,128)S(1)}, s32[1,8]{1,0:T(1,128)}, u32[]{:S(2)}) copy-start(s32[1,8]{1,0:T(1,128)} %param.13) | copy-start | bytes 100
  80.5 10.6 %all-to-all-start.1 = ((bf16[8,2,32,256]{3,2,1,0:T(8,128)(2,1)}), bf16[8,2,32,256]{3,2,1,0:T(8,128)(2,1)S(1)}, u32[]{:S(2)}, u32[]{:S(2)}) async-start(bf16[8,2,32,256]{3,2,1,0:T(8,128)(2,1)} %copy.56), calls=%async_computation.2 | async-start | bytes 524288 | tf_op jit(solution)/shard_map/all_to_all | solution.py:106
  84.2 32.9 %all-gather.4.cloned.1.call-start = ((), (), s32[]{:S(2)}) async-start(), calls=%async_computation.7 | async-start | bytes 1310720 | tf_op jit(solution)/shard_map/all_gather | solution.py:119
  92.2 73.8 %reduce-scatter.5.cloned.1.call-start = ((), (), s32[]{:S(2)}) async-start(), calls=%async_computation.6 | async-start | bytes 2621440 | tf_op jit(solution)/shard_map/reduce_scatter | solution.py:126
  118.5 1.6 copy-start.2
  167.7 10.6 %all-to-all-start.2 = ((f32[8,32,256]{2,1,0:T(8,128)}), f32[8,32,256]{2,1,0:T(8,128)S(1)}, u32[]{:S(2)}, u32[]{:S(2)}) async-start(f32[8,32,256]{2,1,0:T(8,128)} %bitcast.38), calls=%async_computation.4 | async-start | bytes 524288 | tf_op jit(solution)/shard_map/all_to_all | solution.py:106
Sparse Core Ops, SparseCore 0:
  49.6 28.5 reduce-scatter.2
  92.3 24.7 all-gather.3
  122.5 43.3 reduce-scatter.4

commit v2 on v1

v2 whole, which is shorter than its diff:
```python
import jax
import jax.numpy as jnp
from jax import lax
from jax.experimental import pallas as pl
from jax.experimental.pallas import tpu as pltpu
from jax.sharding import PartitionSpec as P

LAYERS = 2
CHUNK = 16


def dense_kernel(slots_ref, cols_ref, count_ref, vals_ref, out_ref, acc):
    turn = pl.program_id(0)
    groups, sources, size, _ = acc.shape
    width, _, part, _ = out_ref.shape

    @pl.when(turn == 0)
    def _():
        acc[...] = jnp.zeros_like(acc)

    begin = turn * CHUNK
    live = jnp.clip(count_ref[0] - begin, 0, CHUNK)

    def add(b, carry):
        s, c = slots_ref[begin + b], cols_ref[begin + b]
        acc[s, c] += vals_ref[b].astype(jnp.float32)
        return carry

    lax.fori_loop(0, live, add, 0)

    @pl.when(turn == pl.num_programs(0) - 1)
    def _():
        def put(s, carry):
            for c in range(sources):
                for e in range(width):
                    out_ref[e, s, :, c * size:(c + 1) * size] = acc[
                        s, c, e * part:(e + 1) * part, :
                    ].astype(out_ref.dtype)
            return carry

        lax.fori_loop(0, groups, put, 0)


def dense_adjacency(vals, slots, cols, count, groups, sources, width):
    total, size, _ = vals.shape
    part = size // width
    return pl.pallas_call(
        dense_kernel,
        out_shape=jax.ShapeDtypeStruct((width, groups, part, sources * size), jnp.bfloat16),
        grid_spec=pltpu.PrefetchScalarGridSpec(
            num_scalar_prefetch=3,
            grid=(total // CHUNK,),
            in_specs=[pl.BlockSpec((CHUNK, size, size), lambda t, *_: (t, 0, 0))],
            out_specs=pl.BlockSpec(
                (width, groups, part, sources * size), lambda t, *_: (0, 0, 0, 0)
            ),
            scratch_shapes=[pltpu.VMEM((groups, sources, size, size), jnp.float32)],
        ),
        compiler_params=pltpu.CompilerParams(
            dimension_semantics=("arbitrary",), vmem_limit_bytes=56 * 1024 * 1024
        ),
    )(slots, cols, count, vals)


def layers_kernel(dense, source, embed_share, cot_share, outgoing, slots, hits,
                  final, grad,
                  asked0, asked1, layers, source2, got_f1, send_b1,
                  sum_f1, land_f1, sum_b1, land_b1, sum_f2, land_f2, sum_b2, land_b2, got_f2,
                  node_sems, line_sems):
    nodes, width = lax.axis_size("node"), lax.axis_size("edge")
    me, z = lax.axis_index("node"), lax.axis_index("edge")
    groups, part, depth = outgoing.shape
    sources = embed_share.shape[0]
    size = part * width
    f32, bf16 = jnp.float32, jnp.bfloat16

    barrier = pltpu.get_barrier_semaphore()

    def greet(k, carry):
        pl.semaphore_signal(barrier, inc=1, device_id={"node": lax.rem(me + k, nodes)},
                            device_id_type=pl.DeviceIdType.MESH)
        return carry

    lax.fori_loop(1, nodes, greet, 0)

    @pl.when(z > 0)
    def _():
        pl.semaphore_signal(barrier, inc=1, device_id={"edge": z - 1},
                            device_id_type=pl.DeviceIdType.MESH)

    @pl.when(z < width - 1)
    def _():
        pl.semaphore_signal(barrier, inc=1, device_id={"edge": z + 1},
                            device_id_type=pl.DeviceIdType.MESH)

    above = jnp.where(z < width - 1, 1, 0)
    below = jnp.where(z > 0, 1, 0)
    pl.semaphore_wait(barrier, nodes - 1 + above + below)

    class Exchange:
        def __init__(self, at, out, into):
            self.at, self.out, self.into = at, out, into

        def copy(self, k, src, dst, peer):
            return pltpu.make_async_remote_copy(
                src_ref=src, dst_ref=dst,
                send_sem=node_sems.at[self.at, 0, k], recv_sem=node_sems.at[self.at, 1, k],
                device_id={"node": peer}, device_id_type=pl.DeviceIdType.MESH)

        def start(self):
            def go(k, carry):
                peer = lax.rem(me + k, nodes)
                self.copy(k, self.out(peer), self.into(me), peer).start()
                return carry

            lax.fori_loop(1, nodes, go, 0)
            self.into(me)[...] = self.out(me)[...]

        def wait(self):
            def go(k, carry):
                peer = lax.rem(me + nodes - k, nodes)
                self.copy(k, self.into(peer), self.into(peer), peer).wait_recv()
                return carry

            lax.fori_loop(1, nodes, go, 0)

        def end(self):
            def go(k, carry):
                peer = lax.rem(me + k, nodes)
                self.copy(k, self.out(peer), self.into(me), peer).wait_send()
                return carry

            lax.fori_loop(1, nodes, go, 0)

    def line_copy(at, way, t, src, dst):
        return pltpu.make_async_remote_copy(
            src_ref=src, dst_ref=dst,
            send_sem=line_sems.at[at, 0, way, t], recv_sem=line_sems.at[at, 1, way, t],
            device_id={"edge": z + 1 if way == 0 else z - 1},
            device_id_type=pl.DeviceIdType.MESH)

    class Gather:
        def __init__(self, at, buf):
            self.at, self.buf = at, buf

        def send(self, way, t):
            chunk = self.buf.at[z - t if way == 0 else z + t]
            return line_copy(self.at, way, t, chunk, chunk)

        def sends(self, way, t):
            return ((z - t >= 0) & (z < width - 1)) if way == 0 else ((z + t < width) & (z > 0))

        def start(self):
            for way in range(2):
                @pl.when(self.sends(way, 0))
                def _(way=way):
                    self.send(way, 0).start()

        def step(self, t):
            for way in range(2):
                there = z - 1 - t if way == 0 else z + 1 + t

                @pl.when((there >= 0) if way == 0 else (there < width))
                def _(way=way, there=there):
                    chunk = self.buf.at[there]
                    line_copy(self.at, way, t, chunk, chunk).wait_recv()

                if t + 1 < width - 1:
                    @pl.when(self.sends(way, t + 1))
                    def _(way=way):
                        self.send(way, t + 1).start()

        def end(self):
            for t in range(width - 1):
                for way in range(2):
                    @pl.when(self.sends(way, t))
                    def _(way=way, t=t):
                        self.send(way, t).wait_send()

    class Reduce:
        def __init__(self, at, sums, land):
            self.at, self.sums, self.land = at, sums, land

        def chunk(self, way, t):
            return width - 1 - t if way == 0 else t

        def send(self, way, t):
            return line_copy(self.at, way, t, self.sums.at[self.chunk(way, t)],
                             self.land.at[way, t])

        def sends(self, way, t):
            d = self.chunk(way, t)
            return z < d if way == 0 else z > d

        def start(self):
            for way, first in ((0, 0), (1, width - 1)):
                @pl.when(z == first)
                def _(way=way):
                    for t in range(width - 1):
                        self.send(way, t).start()

        def step(self, t):
            for way in range(2):
                d = self.chunk(way, t)

                @pl.when(((z > 0) & (d >= z)) if way == 0 else ((z < width - 1) & (d <= z)))
                def _(way=way, d=d):
                    line_copy(self.at, way, t, self.sums.at[d], self.land.at[way, t]).wait_recv()
                    total = self.sums[d].astype(f32) + self.land[way, t].astype(f32)
                    self.sums[d] = total.astype(self.sums.dtype)

                @pl.when(((z > 0) & (z < d)) if way == 0 else ((z < width - 1) & (z > d)))
                def _(way=way):
                    self.send(way, t).start()

        def end(self):
            for t in range(width - 1):
                for way in range(2):
                    @pl.when(self.sends(way, t))
                    def _(way=way, t=t):
                        self.send(way, t).wait_send()

    def forward(x_ref, sums):
        x = x_ref[...]
        for e in range(width):
            out = jnp.dot(dense[e].reshape(groups * part, sources * size), x,
                          preferred_element_type=f32)
            sums[e] = out.reshape(groups, part, depth).astype(sums.dtype)

    def backward(asked, sums):
        y = asked[...].reshape(width * groups * part, depth)
        step = 2 * size
        for c in range(0, sources * size, step):
            a = dense[:, :, :, c:c + step].reshape(width * groups * part, step)
            out = lax.dot_general(a, y, (((0,), (0,)), ((), ())), preferred_element_type=f32)
            for g in range(2):
                for e in range(width):
                    begin = g * size + e * part
                    sums[e, c // size + g] = out[begin:begin + part].astype(sums.dtype)

    def placed(got, r):
        total = jnp.zeros((part, depth), f32)
        for i in range(groups):
            total = total + hits[r, i] * got[i].astype(f32)
        return total

    steps = range(width - 1)
    third = float(LAYERS + 1)

    ask0 = Exchange(0, lambda g: outgoing.at[g], lambda g: asked0.at[z, g])
    swap_f1 = Exchange(1, lambda g: sum_f1.at[z, g], lambda g: got_f1.at[g])
    ask1 = Exchange(2, lambda g: send_b1.at[g], lambda g: asked1.at[z, g])
    swap_f2 = Exchange(3, lambda g: sum_f2.at[z, g], lambda g: got_f2.at[g])
    red_f1, all_0 = Reduce(0, sum_f1, land_f1), Gather(1, asked0)
    red_b1, all_f = Reduce(2, sum_b1, land_b1), Gather(3, layers)
    red_f2, all_b = Reduce(4, sum_f2, land_f2), Gather(5, asked1)
    red_b2 = Reduce(6, sum_b2, land_b2)

    ask0.start()
    forward(source, sum_f1)
    red_f1.start()
    ask0.wait()
    all_0.start()
    for t in steps:
        red_f1.step(t)
        all_0.step(t)
    swap_f1.start()

    backward(asked0, sum_b1)
    red_b1.start()
    swap_f1.wait()

    def put_layer(r, carry):
        layers[z, r] = placed(got_f1, r).astype(bf16)
        return carry

    lax.fori_loop(0, sources, put_layer, 0)
    all_f.start()
    for t in steps:
        red_b1.step(t)
        all_f.step(t)

    for i in range(groups):
        send_b1[i] = sum_b1[z, slots[i]]
    ask1.start()

    for e in range(width):
        for g in range(sources):
            source2[g * size + e * part:g * size + (e + 1) * part, :] = layers[e, g]
    forward(source2, sum_f2)
    red_f2.start()
    ask1.wait()
    all_b.start()
    for t in steps:
        red_f2.step(t)
        all_b.step(t)
    swap_f2.start()

    backward(asked1, sum_b2)
    red_b2.start()
    swap_f2.wait()

    def put_final(r, carry):
        total = embed_share[r].astype(f32) + layers[z, r].astype(f32) + placed(got_f2, r)
        final[r] = (total / third).astype(bf16)
        return carry

    lax.fori_loop(0, sources, put_final, 0)
    for t in steps:
        red_b2.step(t)

    def put_grad(r, carry):
        total = cot_share[r].astype(f32) + sum_b1[z, r].astype(f32) + sum_b2[z, r]
        grad[r] = (total / third).astype(bf16)
        return carry

    lax.fori_loop(0, sources, put_grad, 0)
    for sent in (ask0, swap_f1, ask1, swap_f2, red_f1, all_0, red_b1, all_f, red_f2, all_b, red_b2):
        sent.end()


def shards(embed, cotangent, values, block_slot, block_col, block_count, slot_rows):
    width = lax.axis_size("edge")
    nodes = lax.axis_size("node")
    place = lax.axis_index("edge")
    groups = slot_rows.shape[1]
    vals = values[0, 0]
    size = vals.shape[1]
    part = size // width
    sources = embed.shape[0] // size
    depth = embed.shape[1]
    slot_index = slot_rows[0]

    dense = dense_adjacency(
        vals, block_slot[0, 0], block_col[0, 0], block_count[0], groups, sources, width
    )

    def share_of(rows):
        rows = lax.dynamic_slice_in_dim(rows, place * (sources * part), sources * part, 0)
        return rows.reshape(part, sources, depth).transpose(1, 0, 2)

    embed_share, cot_share = share_of(embed), share_of(cotangent)
    outgoing = cot_share[slot_index]
    source = embed.reshape(size, sources, depth).transpose(1, 0, 2).reshape(-1, depth)
    hits = slot_index[None, :] == jnp.arange(sources, dtype=jnp.int32)[:, None]

    f32, bf16 = jnp.float32, jnp.bfloat16
    vmem = pl.BlockSpec(memory_space=pltpu.VMEM)
    smem = pl.BlockSpec(memory_space=pltpu.SMEM)
    by_group, by_source = (groups, part, depth), (sources, part, depth)

    def sums(shape, kind):
        return [pltpu.VMEM((width,) + shape, kind), pltpu.VMEM((2, width - 1) + shape, kind)]

    final, grad = pl.pallas_call(
        layers_kernel,
        out_shape=[jax.ShapeDtypeStruct(by_source, bf16)] * 2,
        in_specs=[vmem] * 5 + [smem] * 2,
        out_specs=[vmem] * 2,
        scratch_shapes=[
            pltpu.VMEM((width,) + by_group, bf16),
            pltpu.VMEM((width,) + by_group, bf16),
            pltpu.VMEM((width,) + by_source, bf16),
            pltpu.VMEM((sources * size, depth), bf16),
            pltpu.VMEM(by_group, bf16),
            pltpu.VMEM(by_group, bf16),
        ]
        + sums(by_group, bf16) + sums(by_source, bf16)
        + sums(by_group, f32) + sums(by_source, f32)
        + [
            pltpu.VMEM(by_group, f32),
            pltpu.SemaphoreType.DMA((4, 2, nodes)),
            pltpu.SemaphoreType.DMA((7, 2, 2, width - 1)),
        ],
        compiler_params=pltpu.CompilerParams(
            collective_id=0, has_side_effects=True, vmem_limit_bytes=56 * 1024 * 1024
        ),
    )(dense, source, embed_share, cot_share, outgoing, slot_index, hits.astype(f32))

    def in_order(blocks):
        return blocks.transpose(1, 0, 2).reshape(part * sources, depth)

    return in_order(final), in_order(grad)


def solution(mesh):
    placed = (
        P("node", None),
        P("node", None),
        P("node", "edge", None, None, None),
        P("node", "edge", None),
        P("node", "edge", None),
        P("node", "edge"),
        P("node", None),
    )
    return jax.shard_map(
        shards,
        mesh=mesh,
        in_specs=placed,
        out_specs=(P(("node", "edge"), None), P(("node", "edge"), None)),
        check_vma=False,
    )
```

time: 187 us -> 148 us (0.79)
  the two profiles are of different devices: /device:TPU:0 before, /device:TPU:8 now
where the time goes in v2:
time: 148 us
  Pallas kernels  136 us (92%)
  local copies, waits for them, and re-layouts  8.11 us (5%)
  other arithmetic  1.92 us (1%)
    pallas_call x1, Pallas kernels, shards(): pl.pallas_call(layers_kernel, out_shape=[jax.ShapeDtypeStruct(by_source,...  128 us
    pallas_call x1, Pallas kernels, dense_adjacency(): pl.pallas_call(dense_kernel, out_shape=jax.ShapeDtypeStruct((width, group...  8 us
    transpose x2, local copies, waits for them, and re-layouts, in_order(): return blocks.transpose(1, 0, 2).reshape(part * sources, depth)  3.27 us

profile of v2, /device:TPU:8, one launch (start us, length us, event | category | flops | bytes accessed | tf_op | source)
XLA Modules:
  0.0 147.5 jit_solution(8404860318812858713)
XLA Ops:
  1.3 0.7 fusion.1
  1.9 1.3 fusion.hits
  3.2 1.0 dynamic-slice_bitcast_fusion
  4.2 0.0 copy-start
  4.2 1.2 gather_fusion
  5.4 0.7 copy.22
  6.1 1.9 %copy.10 = bf16[128,8,256]{2,0,1:T(8,128)(2,1)} copy(bf16[128,8,256]{2,1,0:T(8,128)(2,1)} %bitcast.36) | data formatting | bytes 1048576 | tf_op jit(solution)/shard_map/reshape | solution.py:344
  8.1 8.0 %shard_map.86.dense = bf16[4,8,32,1024]{3,2,1,0:T(8,128)(2,1)} custom-call(s32[128]{0:T(128)} %bitcast.44, s32[128]{0:T(128)} %bitcast.45, s32[1]{0:T(128)} %bitcast.31.count_ref, bf16[128,128,128]{2,1,0:T(8,128)(2,1)} %bitcast.32), custom_call_target="tpu_custom_call" | custom-call | tf_op jit(solution)/shard_map/pallas_call | solution.py:47
  16.1 0.0 copy-done
  16.1 128.2 %shard_map.87 = (bf16[8,32,256]{2,1,0:T(8,128)(2,1)}, bf16[8,32,256]{2,1,0:T(8,128)(2,1)}) custom-call(bf16[4,8,32,1024]{3,2,1,0:T(8,128)(2,1)} %shard_map.86.dense, bf16[1024,256]{1,0:T(8,128)(2,1)} %bitcast.33, bf16[8,32,256]{2,1,0:T(8,128)(2,1)} %bitcast.37, bf16[8,32,256]{2,1,0:T(8,128)(2,1)} %bitcast.35, bf16[8,32,256]{2,1,0:T(8,128)(2,1)} %gather_fusion, ...), custom_call_target="tpu_custom_call" | custom-call | tf_op jit(solution)/shard_map/pallas_call | solution.py:355
  144.2 1.6 %copy.20 = bf16[32,8,256]{2,1,0:T(8,128)(2,1)} copy(bf16[32,8,256]{2,0,1:T(8,128)(2,1)} %bitcast.41) | data formatting | bytes 262144 | tf_op jit(solution)/shard_map/transpose | solution.py:381
  145.9 1.6 %copy.19 = bf16[32,8,256]{2,1,0:T(8,128)(2,1)} copy(bf16[32,8,256]{2,0,1:T(8,128)(2,1)} %bitcast.39) | data formatting | bytes 262144 | tf_op jit(solution)/shard_map/transpose | solution.py:381
  (2 shorter events, 0.0 us)
Async XLA Ops:
  4.2 11.8 %copy-start = (bf16[32,8,256]{2,0,1:T(8,128)(2,1)}, bf16[32,8,256]{2,0,1:T(8,128)(2,1)S(1)}, u32[]{:S(2)}) copy-start(bf16[32,8,256]{2,0,1:T(8,128)(2,1)S(1)} %copy.21) | copy-start | bytes 393220

commit v3 on v2

--- a/solution.py
+++ b/solution.py
@@ -65,11 +65,11 @@
 def layers_kernel(dense, source, embed_share, cot_share, outgoing, slots, hits,
                   final, grad,
                   asked0, asked1, layers, source2, got_f1, send_b1,
-                  sum_f1, land_f1, sum_b1, land_b1, sum_f2, land_f2, sum_b2, land_b2, got_f2,
+                  sum_f1, land_f1, sum_b1, land_b1, sum_f2, send_f2, land_f2, sum_b2, land_b2, got_f2,
                   node_sems, line_sems):
     nodes, width = lax.axis_size("node"), lax.axis_size("edge")
     me, z = lax.axis_index("node"), lax.axis_index("edge")
-    groups, part, depth = outgoing.shape
+    groups, _, part, depth = outgoing.shape
     sources = embed_share.shape[0]
     size = part * width
     f32, bf16 = jnp.float32, jnp.bfloat16
@@ -83,19 +83,13 @@
 
     lax.fori_loop(1, nodes, greet, 0)
 
-    @pl.when(z > 0)
-    def _():
-        pl.semaphore_signal(barrier, inc=1, device_id={"edge": z - 1},
+    def greet_edge(k, carry):
+        pl.semaphore_signal(barrier, inc=1, device_id={"edge": lax.rem(z + k, width)},
                             device_id_type=pl.DeviceIdType.MESH)
-
-    @pl.when(z < width - 1)
-    def _():
-        pl.semaphore_signal(barrier, inc=1, device_id={"edge": z + 1},
-                            device_id_type=pl.DeviceIdType.MESH)
-
-    above = jnp.where(z < width - 1, 1, 0)
-    below = jnp.where(z > 0, 1, 0)
-    pl.semaphore_wait(barrier, nodes - 1 + above + below)
+        return carry
+
+    lax.fori_loop(1, width, greet_edge, 0)
+    pl.semaphore_wait(barrier, nodes + width - 2)
 
     class Exchange:
         def __init__(self, at, out, into):
@@ -132,100 +126,70 @@
 
             lax.fori_loop(1, nodes, go, 0)
 
-    def line_copy(at, way, t, src, dst):
+    def edge_copy(at, k, src, dst, peer):
         return pltpu.make_async_remote_copy(
             src_ref=src, dst_ref=dst,
-            send_sem=line_sems.at[at, 0, way, t], recv_sem=line_sems.at[at, 1, way, t],
-            device_id={"edge": z + 1 if way == 0 else z - 1},
-            device_id_type=pl.DeviceIdType.MESH)
+            send_sem=line_sems.at[at, 0, k - 1], recv_sem=line_sems.at[at, 1, k - 1],
+            device_id={"edge": peer}, device_id_type=pl.DeviceIdType.MESH)
+
+    def after(k):
+        return lax.rem(z + k, width)
+
+    def before(k):
+        return lax.rem(z + width - k, width)
 
     class Gather:
         def __init__(self, at, buf):
             self.at, self.buf = at, buf
 
-        def send(self, way, t):
-            chunk = self.buf.at[z - t if way == 0 else z + t]
-            return line_copy(self.at, way, t, chunk, chunk)
-
-        def sends(self, way, t):
-            return ((z - t >= 0) & (z < width - 1)) if way == 0 else ((z + t < width) & (z > 0))
+        def send(self, k):
+            return edge_copy(self.at, k, self.buf.at[z], self.buf.at[z], after(k))
 
         def start(self):
-            for way in range(2):
-                @pl.when(self.sends(way, 0))
-                def _(way=way):
-                    self.send(way, 0).start()
+            for k in range(1, width):
+                self.send(k).start()
 
         def step(self, t):
-            for way in range(2):
-                there = z - 1 - t if way == 0 else z + 1 + t
-
-                @pl.when((there >= 0) if way == 0 else (there < width))
-                def _(way=way, there=there):
-                    chunk = self.buf.at[there]
-                    line_copy(self.at, way, t, chunk, chunk).wait_recv()
-
-                if t + 1 < width - 1:
-                    @pl.when(self.sends(way, t + 1))
-                    def _(way=way):
-                        self.send(way, t + 1).start()
+            chunk = self.buf.at[before(t + 1)]
+            edge_copy(self.at, t + 1, chunk, chunk, before(t + 1)).wait_recv()
 
         def end(self):
-            for t in range(width - 1):
-                for way in range(2):
-                    @pl.when(self.sends(way, t))
-                    def _(way=way, t=t):
-                        self.send(way, t).wait_send()
+            for k in range(1, width):
+                self.send(k).wait_send()
 
     class Reduce:
-        def __init__(self, at, sums, land):
+        def __init__(self, at, sums, land, out=None):
             self.at, self.sums, self.land = at, sums, land
-
-        def chunk(self, way, t):
-            return width - 1 - t if way == 0 else t
-
-        def send(self, way, t):
-            return line_copy(self.at, way, t, self.sums.at[self.chunk(way, t)],
-                             self.land.at[way, t])
-
-        def sends(self, way, t):
-            d = self.chunk(way, t)
-            return z < d if way == 0 else z > d
+            self.out = sums if out is None else out
+
+        def send(self, k):
+            return edge_copy(self.at, k, self.out.at[after(k)], self.land.at[k - 1], after(k))
 
         def start(self):
-            for way, first in ((0, 0), (1, width - 1)):
-                @pl.when(z == first)
-                def _(way=way):
-                    for t in range(width - 1):
-                        self.send(way, t).start()
+            for k in range(1, width):
+                self.send(k).start()
 
         def step(self, t):
-            for way in range(2):
-                d = self.chunk(way, t)
-
-                @pl.when(((z > 0) & (d >= z)) if way == 0 else ((z < width - 1) & (d <= z)))
-                def _(way=way, d=d):
-                    line_copy(self.at, way, t, self.sums.at[d], self.land.at[way, t]).wait_recv()
-                    total = self.sums[d].astype(f32) + self.land[way, t].astype(f32)
-                    self.sums[d] = total.astype(self.sums.dtype)
-
-                @pl.when(((z > 0) & (z < d)) if way == 0 else ((z < width - 1) & (z > d)))
-                def _(way=way):
-                    self.send(way, t).start()
+            edge_copy(self.at, t + 1, self.land.at[t], self.land.at[t], before(t + 1)).wait_recv()
+            if t == width - 2:
+                total = self.sums[z].astype(f32)
+                for k in range(width - 1):
+                    total = total + self.land[k].astype(f32)
+                self.sums[z] = total.astype(self.sums.dtype)
 
         def end(self):
-            for t in range(width - 1):
-                for way in range(2):
-                    @pl.when(self.sends(way, t))
-                    def _(way=way, t=t):
-                        self.send(way, t).wait_send()
-
-    def forward(x_ref, sums):
+            for k in range(1, width):
+                self.send(k).wait_send()
+
+    def forward(x_ref, sums, wide=None):
         x = x_ref[...]
         for e in range(width):
             out = jnp.dot(dense[e].reshape(groups * part, sources * size), x,
                           preferred_element_type=f32)
-            sums[e] = out.reshape(groups, part, depth).astype(sums.dtype)
+            out = out.reshape(groups, part, depth)
+            sums[e] = out.astype(sums.dtype)
+            if wide is not None:
+                wide[e] = out
 
     def backward(asked, sums):
         y = asked[...].reshape(width * groups * part, depth)
@@ -247,27 +211,27 @@
     steps = range(width - 1)
     third = float(LAYERS + 1)
 
-    ask0 = Exchange(0, lambda g: outgoing.at[g], lambda g: asked0.at[z, g])
+    ask0 = Exchange(0, lambda g: outgoing.at[g], lambda g: asked0.at[:, g])
     swap_f1 = Exchange(1, lambda g: sum_f1.at[z, g], lambda g: got_f1.at[g])
     ask1 = Exchange(2, lambda g: send_b1.at[g], lambda g: asked1.at[z, g])
     swap_f2 = Exchange(3, lambda g: sum_f2.at[z, g], lambda g: got_f2.at[g])
-    red_f1, all_0 = Reduce(0, sum_f1, land_f1), Gather(1, asked0)
-    red_b1, all_f = Reduce(2, sum_b1, land_b1), Gather(3, layers)
-    red_f2, all_b = Reduce(4, sum_f2, land_f2), Gather(5, asked1)
-    red_b2 = Reduce(6, sum_b2, land_b2)
+    red_f1 = Reduce(0, sum_f1, land_f1)
+    red_b1, all_f = Reduce(1, sum_b1, land_b1), Gather(2, layers)
+    red_f2, all_b = Reduce(3, sum_f2, land_f2, send_f2), Gather(4, asked1)
+    red_b2 = Reduce(5, sum_b2, land_b2)
+
+    def arrive(moved):
+        for t in steps:
+            moved.step(t)
 
     ask0.start()
     forward(source, sum_f1)
     red_f1.start()
     ask0.wait()
-    all_0.start()
-    for t in steps:
-        red_f1.step(t)
-        all_0.step(t)
-    swap_f1.start()
-
     backward(asked0, sum_b1)
     red_b1.start()
+    arrive(red_f1)
+    swap_f1.start()
     swap_f1.wait()
 
     def put_layer(r, carry):
@@ -276,28 +240,23 @@
 
     lax.fori_loop(0, sources, put_layer, 0)
     all_f.start()
-    for t in steps:
-        red_b1.step(t)
-        all_f.step(t)
-
+    arrive(red_b1)
     for i in range(groups):
         send_b1[i] = sum_b1[z, slots[i]]
     ask1.start()
-
+    ask1.wait()
+    all_b.start()
+    arrive(all_f)
     for e in range(width):
         for g in range(sources):
             source2[g * size + e * part:g * size + (e + 1) * part, :] = layers[e, g]
-    forward(source2, sum_f2)
+    forward(source2, send_f2, sum_f2)
     red_f2.start()
-    ask1.wait()
-    all_b.start()
-    for t in steps:
-        red_f2.step(t)
-        all_b.step(t)
-    swap_f2.start()
-
+    arrive(all_b)
     backward(asked1, sum_b2)
     red_b2.start()
+    arrive(red_f2)
+    swap_f2.start()
     swap_f2.wait()
 
     def put_final(r, carry):
@@ -306,8 +265,7 @@
         return carry
 
     lax.fori_loop(0, sources, put_final, 0)
-    for t in steps:
-        red_b2.step(t)
+    arrive(red_b2)
 
     def put_grad(r, carry):
         total = cot_share[r].astype(f32) + sum_b1[z, r].astype(f32) + sum_b2[z, r]
@@ -315,7 +273,7 @@
         return carry
 
     lax.fori_loop(0, sources, put_grad, 0)
-    for sent in (ask0, swap_f1, ask1, swap_f2, red_f1, all_0, red_b1, all_f, red_f2, all_b, red_b2):
+    for sent in (ask0, swap_f1, ask1, swap_f2, red_f1, red_b1, all_f, red_f2, all_b, red_b2):
         sent.end()
 
 
@@ -340,7 +298,8 @@
         return rows.reshape(part, sources, depth).transpose(1, 0, 2)
 
     embed_share, cot_share = share_of(embed), share_of(cotangent)
-    outgoing = cot_share[slot_index]
+    blocks = cotangent.reshape(size, sources, depth).transpose(1, 0, 2)
+    outgoing = blocks[slot_index].reshape(groups, width, part, depth)
     source = embed.reshape(size, sources, depth).transpose(1, 0, 2).reshape(-1, depth)
     hits = slot_index[None, :] == jnp.arange(sources, dtype=jnp.int32)[:, None]
 
@@ -350,7 +309,7 @@
     by_group, by_source = (groups, part, depth), (sources, part, depth)
 
     def sums(shape, kind):
-        return [pltpu.VMEM((width,) + shape, kind), pltpu.VMEM((2, width - 1) + shape, kind)]
+        return [pltpu.VMEM((width,) + shape, kind), pltpu.VMEM((width - 1,) + shape, kind)]
 
     final, grad = pl.pallas_call(
         layers_kernel,
@@ -366,11 +325,12 @@
             pltpu.VMEM(by_group, bf16),
         ]
         + sums(by_group, bf16) + sums(by_source, bf16)
-        + sums(by_group, f32) + sums(by_source, f32)
+        + [pltpu.VMEM((width,) + by_group, f32)]
+        + sums(by_group, bf16) + sums(by_source, f32)
         + [
             pltpu.VMEM(by_group, f32),
             pltpu.SemaphoreType.DMA((4, 2, nodes)),
-            pltpu.SemaphoreType.DMA((7, 2, 2, width - 1)),
+            pltpu.SemaphoreType.DMA((6, 2, width - 1)),
         ],
         compiler_params=pltpu.CompilerParams(
             collective_id=0, has_side_effects=True, vmem_limit_bytes=56 * 1024 * 1024

time: 148 us -> 110 us (0.74)
  Pallas kernels: 136 us -> 95.9 us
  local copies, waits for them, and re-layouts: 8.11 us -> 10.1 us
    pallas_call x1, Pallas kernels: 128 us -> 88.4 us  [shards(): pl.pallas_call(layers_kernel, out_shape=[jax.ShapeDtypeStruct(by_source,...]
where the time goes in v3:
time: 110 us; the launch traced here: 109 us
  Pallas kernels  95.9 us (87%)
  local copies, waits for them, and re-layouts  10.1 us (9%)
  other arithmetic  1.92 us (2%)
  between operations  1.3 us (1%)
    pallas_call x1, Pallas kernels, shards(): pl.pallas_call(layers_kernel, out_shape=[jax.ShapeDtypeStruct(by_source,...  88.4 us
    pallas_call x1, Pallas kernels, dense_adjacency(): pl.pallas_call(dense_kernel, out_shape=jax.ShapeDtypeStruct((width, group...  7.43 us
    transpose x2, local copies, waits for them, and re-layouts, in_order(): return blocks.transpose(1, 0, 2).reshape(part * sources, depth)  3.27 us
    reshape x3, local copies, waits for them, and re-layouts, share_of(): return rows.reshape(part, sources, depth).transpose(1, 0, 2)  2.35 us

profile of v3, /device:TPU:8, one launch (start us, length us, event | category | flops | bytes accessed | tf_op | source)
XLA Modules:
  0.0 109.2 jit_solution(452419481625979616)
XLA Ops:
  1.3 0.7 fusion.1
  1.9 1.2 %fusion.hits = f32[8,8]{1,0:T(8,128)} fusion(s32[8]{0:T(128)} %bitcast.49), kind=kLoop, calls=%fused_computation.10 | loop fusion | flops 128 | bytes 288 | tf_op jit(solution)/shard_map/convert_element_type | solution.py:338
  3.2 1.0 dynamic-slice_bitcast_fusion
  4.2 0.7 copy.29
  4.9 0.7 copy.30
  5.5 1.1 %copy.26 = bf16[128,8,256]{2,0,1:T(8,128)(2,1)S(1)} copy(bf16[128,8,256]{2,1,0:T(8,128)(2,1)} %bitcast.41) | data formatting | bytes 1048576 | tf_op jit(solution)/shard_map/reshape | solution.py:301
  6.7 1.4 %gather_fusion = bf16[8,128,256]{2,1,0:T(8,128)(2,1)} fusion(bf16[8,128,256]{2,1,0:T(8,128)(2,1)S(1)} %bitcast.38, s32[1024]{0:T(1024)S(1)} %pad_clamp_fusion), kind=kCustom, calls=%fused_computation | custom fusion | bytes 1048608 | tf_op jit(solution)/shard_map/gather | solution.py:302
  8.1 1.9 %copy.15 = bf16[128,8,256]{2,0,1:T(8,128)(2,1)} copy(bf16[128,8,256]{2,1,0:T(8,128)(2,1)} %bitcast.42) | data formatting | bytes 1048576 | tf_op jit(solution)/shard_map/reshape | solution.py:303
  10.0 7.4 %shard_map.86.dense = bf16[4,8,32,1024]{3,2,1,0:T(8,128)(2,1)} custom-call(s32[128]{0:T(128)} %bitcast.51, s32[128]{0:T(128)} %bitcast.52, s32[1]{0:T(128)} %bitcast.36.count_ref, bf16[128,128,128]{2,1,0:T(8,128)(2,1)} %bitcast.37), custom_call_target="tpu_custom_call" | custom-call | tf_op jit(solution)/shard_map/pallas_call | solution.py:47
  17.4 88.4 %shard_map.87 = (bf16[8,32,256]{2,1,0:T(8,128)(2,1)}, bf16[8,32,256]{2,1,0:T(8,128)(2,1)}) custom-call(bf16[4,8,32,1024]{3,2,1,0:T(8,128)(2,1)} %shard_map.86.dense, bf16[1024,256]{1,0:T(8,128)(2,1)} %bitcast.39, bf16[8,32,256]{2,1,0:T(8,128)(2,1)} %bitcast.44, bf16[8,32,256]{2,1,0:T(8,128)(2,1)} %bitcast.43, bf16[8,4,32,256]{3,2,1,0:T(8,128)(2,1)} %bitcast.40, ...), custom_call_target="tpu_custom_call" | custom-call | tf_op jit(solution)/shard_map/pallas_call | solution.py:314
  105.9 1.6 %copy.28 = bf16[32,8,256]{2,1,0:T(8,128)(2,1)} copy(bf16[32,8,256]{2,0,1:T(8,128)(2,1)} %bitcast.48) | data formatting | bytes 262144 | tf_op jit(solution)/shard_map/transpose | solution.py:341
  107.5 1.6 %copy.27 = bf16[32,8,256]{2,1,0:T(8,128)(2,1)} copy(bf16[32,8,256]{2,0,1:T(8,128)(2,1)} %bitcast.46) | data formatting | bytes 262144 | tf_op jit(solution)/shard_map/transpose | solution.py:341
  (1 shorter events, 0.0 us)

commit v4 on v3

--- a/solution.py
+++ b/solution.py
@@ -65,7 +65,8 @@
 def layers_kernel(dense, source, embed_share, cot_share, outgoing, slots, hits,
                   final, grad,
                   asked0, asked1, layers, source2, got_f1, send_b1,
-                  sum_f1, land_f1, sum_b1, land_b1, sum_f2, send_f2, land_f2, sum_b2, land_b2, got_f2,
+                  sum_f1, land_f1, sum_b1, land_b1, sum_f2, send_f2, land_f2, sum_b2, send_b2, land_b2,
+                  mean_f2, land_mf2, mean_b2, land_mb2, got_f2,
                   node_sems, line_sems):
     nodes, width = lax.axis_size("node"), lax.axis_size("edge")
     me, z = lax.axis_index("node"), lax.axis_index("edge")
@@ -181,17 +182,20 @@
             for k in range(1, width):
                 self.send(k).wait_send()
 
-    def forward(x_ref, sums, wide=None):
+    def forward(x_ref, sums, wide=None, means=None):
         x = x_ref[...]
         for e in range(width):
             out = jnp.dot(dense[e].reshape(groups * part, sources * size), x,
                           preferred_element_type=f32)
             out = out.reshape(groups, part, depth)
+            if wide is not None:
+                middle = jnp.mean(out, axis=1)
+                means[e] = middle
+                out = out - middle[:, None, :]
+                wide[e] = out
             sums[e] = out.astype(sums.dtype)
-            if wide is not None:
-                wide[e] = out
-
-    def backward(asked, sums):
+
+    def backward(asked, sums, wide=None, means=None):
         y = asked[...].reshape(width * groups * part, depth)
         step = 2 * size
         for c in range(0, sources * size, step):
@@ -200,7 +204,13 @@
             for g in range(2):
                 for e in range(width):
                     begin = g * size + e * part
-                    sums[e, c // size + g] = out[begin:begin + part].astype(sums.dtype)
+                    block = out[begin:begin + part]
+                    if wide is not None:
+                        middle = jnp.mean(block, axis=0, keepdims=True)
+                        means[e, c // size + g:c // size + g + 1, :] = middle
+                        block = block - middle
+                        wide[e, c // size + g] = block
+                    sums[e, c // size + g] = block.astype(sums.dtype)
 
     def placed(got, r):
         total = jnp.zeros((part, depth), f32)
@@ -218,7 +228,8 @@
     red_f1 = Reduce(0, sum_f1, land_f1)
     red_b1, all_f = Reduce(1, sum_b1, land_b1), Gather(2, layers)
     red_f2, all_b = Reduce(3, sum_f2, land_f2, send_f2), Gather(4, asked1)
-    red_b2 = Reduce(5, sum_b2, land_b2)
+    red_b2 = Reduce(5, sum_b2, land_b2, send_b2)
+    mid_f2, mid_b2 = Reduce(6, mean_f2, land_mf2), Reduce(7, mean_b2, land_mb2)
 
     def arrive(moved):
         for t in steps:
@@ -250,12 +261,16 @@
     for e in range(width):
         for g in range(sources):
             source2[g * size + e * part:g * size + (e + 1) * part, :] = layers[e, g]
-    forward(source2, send_f2, sum_f2)
+    forward(source2, send_f2, sum_f2, mean_f2)
+    mid_f2.start()
     red_f2.start()
     arrive(all_b)
-    backward(asked1, sum_b2)
+    backward(asked1, send_b2, sum_b2, mean_b2)
+    mid_b2.start()
     red_b2.start()
+    arrive(mid_f2)
     arrive(red_f2)
+    sum_f2[z] = sum_f2[z] + mean_f2[z][:, None, :]
     swap_f2.start()
     swap_f2.wait()
 
@@ -265,7 +280,9 @@
         return carry
 
     lax.fori_loop(0, sources, put_final, 0)
+    arrive(mid_b2)
     arrive(red_b2)
+    sum_b2[z] = sum_b2[z] + mean_b2[z][:, None, :]
 
     def put_grad(r, carry):
         total = cot_share[r].astype(f32) + sum_b1[z, r].astype(f32) + sum_b2[z, r]
@@ -273,7 +290,7 @@
         return carry
 
     lax.fori_loop(0, sources, put_grad, 0)
-    for sent in (ask0, swap_f1, ask1, swap_f2, red_f1, red_b1, all_f, red_f2, all_b, red_b2):
+    for sent in (ask0, swap_f1, ask1, swap_f2, red_f1, red_b1, all_f, red_f2, all_b, red_b2, mid_f2, mid_b2):
         sent.end()
 
 
@@ -326,11 +343,13 @@
         ]
         + sums(by_group, bf16) + sums(by_source, bf16)
         + [pltpu.VMEM((width,) + by_group, f32)]
-        + sums(by_group, bf16) + sums(by_source, f32)
+        + sums(by_group, bf16) + [pltpu.VMEM((width,) + by_source, f32)]
+        + sums(by_source, bf16)
+        + sums((groups, depth), f32) + sums((sources, depth), f32)
         + [
             pltpu.VMEM(by_group, f32),
             pltpu.SemaphoreType.DMA((4, 2, nodes)),
-            pltpu.SemaphoreType.DMA((6, 2, width - 1)),
+            pltpu.SemaphoreType.DMA((8, 2, width - 1)),
         ],
         compiler_params=pltpu.CompilerParams(
             collective_id=0, has_side_effects=True, vmem_limit_bytes=56 * 1024 * 1024

time: 110 us -> 99.9 us (0.908)
  Pallas kernels: 95.9 us -> 86.2 us
    pallas_call x1, Pallas kernels: 88.4 us -> 78.6 us  [shards(): pl.pallas_call(layers_kernel, out_shape=[jax.ShapeDtypeStruct(by_source,...]
where the time goes in v4:
time: 99.9 us; the launch traced here: 99.5 us
  Pallas kernels  86.2 us (86%)
  local copies, waits for them, and re-layouts  10.1 us (10%)
  other arithmetic  1.92 us (2%)
  between operations  1.3 us (1%)
    pallas_call x1, Pallas kernels, shards(): pl.pallas_call(layers_kernel, out_shape=[jax.ShapeDtypeStruct(by_source,...  78.6 us
    pallas_call x1, Pallas kernels, dense_adjacency(): pl.pallas_call(dense_kernel, out_shape=jax.ShapeDtypeStruct((width, group...  7.63 us
    transpose x2, local copies, waits for them, and re-layouts, in_order(): return blocks.transpose(1, 0, 2).reshape(part * sources, depth)  3.27 us
    reshape x3, local copies, waits for them, and re-layouts, share_of(): return rows.reshape(part, sources, depth).transpose(1, 0, 2)  2.35 us

profile of v4, /device:TPU:8, one launch (start us, length us, event | category | flops | bytes accessed | tf_op | source)
XLA Modules:
  0.0 99.5 jit_solution(9455244927175531475)
XLA Ops:
  1.3 0.7 fusion.1
  1.9 1.2 %fusion.hits = f32[8,8]{1,0:T(8,128)} fusion(s32[8]{0:T(128)} %bitcast.49), kind=kLoop, calls=%fused_computation.10 | loop fusion | flops 128 | bytes 288 | tf_op jit(solution)/shard_map/convert_element_type | solution.py:357
  3.2 1.0 dynamic-slice_bitcast_fusion
  4.2 0.7 copy.29
  4.9 0.7 copy.30
  5.5 1.1 %copy.26 = bf16[128,8,256]{2,0,1:T(8,128)(2,1)S(1)} copy(bf16[128,8,256]{2,1,0:T(8,128)(2,1)} %bitcast.41) | data formatting | bytes 1048576 | tf_op jit(solution)/shard_map/reshape | solution.py:318
  6.7 1.4 %gather_fusion = bf16[8,128,256]{2,1,0:T(8,128)(2,1)} fusion(bf16[8,128,256]{2,1,0:T(8,128)(2,1)S(1)} %bitcast.38, s32[1024]{0:T(1024)S(1)} %pad_clamp_fusion), kind=kCustom, calls=%fused_computation | custom fusion | bytes 1048608 | tf_op jit(solution)/shard_map/gather | solution.py:319
  8.1 1.9 %copy.15 = bf16[128,8,256]{2,0,1:T(8,128)(2,1)} copy(bf16[128,8,256]{2,1,0:T(8,128)(2,1)} %bitcast.42) | data formatting | bytes 1048576 | tf_op jit(solution)/shard_map/reshape | solution.py:320
  10.0 7.6 %shard_map.86.dense = bf16[4,8,32,1024]{3,2,1,0:T(8,128)(2,1)} custom-call(s32[128]{0:T(128)} %bitcast.51, s32[128]{0:T(128)} %bitcast.52, s32[1]{0:T(128)} %bitcast.36.count_ref, bf16[128,128,128]{2,1,0:T(8,128)(2,1)} %bitcast.37), custom_call_target="tpu_custom_call" | custom-call | tf_op jit(solution)/shard_map/pallas_call | solution.py:47
  17.6 78.6 %shard_map.87 = (bf16[8,32,256]{2,1,0:T(8,128)(2,1)}, bf16[8,32,256]{2,1,0:T(8,128)(2,1)}) custom-call(bf16[4,8,32,1024]{3,2,1,0:T(8,128)(2,1)} %shard_map.86.dense, bf16[1024,256]{1,0:T(8,128)(2,1)} %bitcast.39, bf16[8,32,256]{2,1,0:T(8,128)(2,1)} %bitcast.44, bf16[8,32,256]{2,1,0:T(8,128)(2,1)} %bitcast.43, bf16[8,4,32,256]{3,2,1,0:T(8,128)(2,1)} %bitcast.40, ...), custom_call_target="tpu_custom_call" | custom-call | tf_op jit(solution)/shard_map/pallas_call | solution.py:331
  96.2 1.6 %copy.28 = bf16[32,8,256]{2,1,0:T(8,128)(2,1)} copy(bf16[32,8,256]{2,0,1:T(8,128)(2,1)} %bitcast.48) | data formatting | bytes 262144 | tf_op jit(solution)/shard_map/transpose | solution.py:360
  97.8 1.6 %copy.27 = bf16[32,8,256]{2,1,0:T(8,128)(2,1)} copy(bf16[32,8,256]{2,0,1:T(8,128)(2,1)} %bitcast.46) | data formatting | bytes 262144 | tf_op jit(solution)/shard_map/transpose | solution.py:360
  (1 shorter events, 0.0 us)
